TPU v7x, 32 devices: a whole 2x2x4 slice. The times are simulated.
32 devices in a mesh: prow: 4 (over y, core), pcol: 8 (over z, x).
Axes of the slice: x: 2, y: 2, z: 4, core: 2. Of those that a mesh axis runs over, the one named last changes fastest.
Arguments:
- parent: float32 [12, 4, 256, 6, 8, 256], P(None, 'prow', None, None, 'pcol')
- children: float32 [8, 4, 256, 2, 8, 256], P(None, 'prow', None, None, 'pcol')
- index_maps: int32 [2, 16], replicated, may hold values from 0 to 47, as said below
Outputs:
- factored: float32 [12, 4, 256, 6, 8, 256], P(None, 'prow', None, None, 'pcol')
Inputs may be any that keep to these rules, and one draw needn't show every extreme that they name: `index_maps`: entry (k, u) is 3 u, 3 u + 1 or 3 u + 2, so each row rises strictly. Of the blocks u of one child with one remainder modulo 2, at most 4 go to parent blocks of one remainder modulo 2 * 2.
All inputs are finite; a program needn't handle non-finite values.
Results may differ from a plain program's by a relative error of at most 0.00005.
Values sent between devices are 32-bit elements; how exact they have to be, the bound alone decides.
A program may use at most 192 MiB of HBM per device.

v0:
```python
import jax
import jax.numpy as jnp
from jax import lax
from jax.sharding import PartitionSpec as P

KB = 5


def broadcast(array, axis, root):
    mine = lax.axis_index(axis) == root
    return lax.psum(jnp.where(mine, array, jnp.zeros_like(array)), axis)


def per_device(parent, children, index_maps):
    prow_count = lax.axis_size("prow")
    pcol_count = lax.axis_size("pcol")
    prow_id = lax.axis_index("prow")
    pcol_id = lax.axis_index("pcol")
    half_grid = prow_count // 2
    block_size = parent.shape[2]
    local_rows = parent.shape[0]
    local_cols = parent.shape[3]
    child_rows = children.shape[0]
    child_cols = children.shape[3]
    child_blocks = index_maps.shape[1]
    highest = lax.Precision.HIGHEST
    child_id = prow_id // half_grid
    residue = prow_id % half_grid
    child_map = jnp.where(child_id == 0, index_maps[0], index_maps[1])
    col_ids = jnp.arange(local_cols) * pcol_count + pcol_id
    row_ids = jnp.arange(local_rows) * prow_count + prow_id
    shard_piece = lax.all_gather(children, "pcol", axis=4, tiled=True)
    piece_cols = shard_piece.shape[4]
    col_index = jnp.arange(child_cols)[:, None] * pcol_count + jnp.arange(piece_cols)[None, :]
    mapped = jnp.sum(
        jnp.where(
            col_index[:, :, None] == jnp.arange(child_blocks)[None, None, :],
            child_map[None, None, :],
            0,
        ),
        axis=2,
    )
    select = (mapped[None, :, :] == col_ids[:, None, None]).astype(jnp.float32)
    sectioning = jnp.einsum("luq,rauqb->ralb", select, shard_piece[:, 0], precision=highest)
    row_index = jnp.arange(child_rows) * half_grid + residue
    target = jnp.sum(
        jnp.where(row_index[:, None] == jnp.arange(child_blocks)[None, :], child_map[None, :], 0),
        axis=1,
    )
    target_row = target % prow_count
    slot_row = target // prow_count
    earlier = jnp.arange(child_rows)[:, None] > jnp.arange(child_rows)[None, :]
    position = jnp.sum(earlier & (target_row[:, None] == target_row[None, :]), axis=1)
    most_rows = (child_rows // 2 + 2) // 3 * (2 - min(1, half_grid // 3))
    placed = (target_row[None, None, :] == jnp.arange(prow_count)[:, None, None]) & (
        position[None, None, :] == jnp.arange(most_rows)[None, :, None]
    )
    placement = placed.astype(jnp.float32)
    labels = jnp.sum(jnp.where(placed, slot_row[None, None, :] + 1, 0), axis=2) - 1
    own_front = parent[:, 0, :, :, 0, :]
    received = lax.all_to_all(
        jnp.einsum("dsr,ralb->dsalb", placement, sectioning, precision=highest),
        "prow",
        split_axis=0,
        concat_axis=0,
        tiled=True,
    )
    got_labels = lax.all_to_all(labels, "prow", split_axis=0, concat_axis=0, tiled=True)
    select = (got_labels[None, :, :] == jnp.arange(local_rows)[:, None, None]).astype(jnp.float32)
    front_block = own_front + jnp.einsum("lps,psacb->lacb", select, received, precision=highest)
    for panel_index in range(KB):
        panel_front_block = front_block
        owner_row = panel_index % prow_count
        owner_col = panel_index % pcol_count
        slot_index = panel_index // prow_count
        diagonal = broadcast(panel_front_block[slot_index, :, 0, :], "prow", owner_row)
        owner_here = pcol_id == owner_col
        diagonal = jnp.where(owner_here, diagonal, jnp.eye(block_size, dtype=jnp.float32))
        factor = jnp.tril(jnp.linalg.cholesky(diagonal))
        column = panel_front_block[:, :, 0, :].reshape(local_rows * block_size, block_size)
        solved = lax.linalg.triangular_solve(
            factor, column, left_side=False, lower=True, transpose_a=True
        )
        solved = solved.reshape(local_rows, block_size, block_size)
        below_rows = jnp.where((row_ids > panel_index)[:, None, None], solved, 0.0)
        new_column = jnp.where((row_ids == panel_index)[:, None, None], factor[None], below_rows)
        panel_front_block = panel_front_block.at[:, :, 0, :].set(
            jnp.where(owner_here, new_column, panel_front_block[:, :, 0, :])
        )
        panel_left = broadcast(below_rows, "pcol", owner_col)
        grouped = panel_left.reshape(local_cols, pcol_count // prow_count, block_size, block_size)
        chosen = lax.dynamic_index_in_dim(grouped, pcol_id // prow_count, 1, keepdims=False)
        panel_right = broadcast(chosen, "prow", pcol_id % prow_count)
        front_block, panel_left, panel_right = (panel_front_block, panel_left, panel_right)
        front_block = front_block - jnp.einsum(
            "rab,ceb->race", panel_left, panel_right, precision=highest
        )
    zero_mask = (row_ids < KB)[:, None, None, None] & (col_ids >= KB)[None, None, :, None]
    front_block = jnp.where(zero_mask, 0.0, front_block)
    return front_block.reshape(local_rows, 1, block_size, local_cols, 1, block_size)


def solution(mesh):
    in_specs = (
        P(None, "prow", None, None, "pcol", None),
        P(None, "prow", None, None, "pcol", None),
        P(),
    )
    out_specs = P(None, "prow", None, None, "pcol", None)
    return jax.shard_map(
        per_device, mesh=mesh, in_specs=in_specs, out_specs=out_specs, check_vma=False
    )
```

profile of v0, /device:TPU:0, one launch (start us, length us, event | category | flops | bytes accessed | tf_op | source)
XLA Modules:
  0.0 2679.6 jit_solution(7912544859046727803)
XLA Ops:
  6.5 4.7 copy.121
  13.0 4.2 all-to-all-start
  17.6 634.3 %all-gather.2.cloned.1.call-done = f32[8,1,256,2,8,256]{5,2,3,1,0,4:T(8,128)} async-done(((f32[8,1,256,2,1,256]{5,2,3,1,0,4:T(8,128)}), f32[8,1,256,2,8,256]{5,2,3,1,0,4:T(8,128)}) %all-gather.2.cloned.1.call-update) | async-done | bytes 33554448 | tf_op jit(solution)/shard_map/all_gather | solution.py:32
  651.8 41.6 %fusion.6 = f32[8,256,6,256]{3,2,1,0:T(8,128)} fusion(f32[8,1,256,2,8,256]{5,2,3,1,0,4:T(8,128)} %all-gather.2.cloned.1.call-done, s32[2,8]{1,0:T(2,128)S(1)} %select_reduce_fusion.10, s32[6]{0:T(128)S(1)} %multiply_add_fusion.1), kind=kOutput, calls=%fused_computation.23 | convolution fusion | flops 603979904 | bytes 46137432 | tf_op jit(solution)/shard_map/luq,rauqb->ralb/dot_general | solution.py:44
  693.4 29.2 %fusion.3 = f32[4,4,256,6,256]{4,1,3,2,0:T(4,128)} fusion(f32[8,256,6,256]{3,2,1,0:T(8,128)} %fusion.6, pred[4,8]{1,0:T(4,128)(4,1)S(1)} %get-tuple-element.198, pred[4,8]{1,0:T(4,128)(4,1)S(1)} %get-tuple-element.199), kind=kOutput, calls=%fused_computation.15 | convolution fusion | flops 603979904 | bytes 37748800 | tf_op jit(solution)/shard_map/dsr,ralb->dsalb/dot_general | solution.py:62
  722.6 8.4 all-to-all-start.1
  731.1 44.7 %copy.119 = f32[12,1,256,6,1,256]{2,5,3,0,4,1:T(8,128)} copy(f32[12,1,256,6,1,256]{5,4,3,2,1,0:T(1,128)} %param.16) | data formatting | bytes 37748736 | tf_op args[0]
  775.9 228.1 %all-to-all-done.1 = f32[4,4,256,6,256]{4,1,3,2,0:T(4,128)} async-done(((f32[4,4,256,6,256]{4,1,3,2,0:T(4,128)}), f32[4,4,256,6,256]{4,1,3,2,0:T(4,128)}, u32[]{:S(2)}, u32[]{:S(2)}) %all-to-all-start.1) | async-done | bytes 25165856 | tf_op jit(solution)/shard_map/all_to_all | solution.py:61
  1004.0 25.4 convolution_bitcast_fusion
  1029.4 23.2 copy.126
  1052.6 12.7 bitcast_add_fusion
  1065.3 6.8 copy-done.4
  1077.7 26.4 all-reduce.17.cloned.1.call-done
  1107.7 11.7 cholesky.256
  1119.4 9.8 custom-call.19
  1131.4 11.7 cholesky.273
  1147.4 3.9 while.15
  1151.9 20.6 custom-call.20
  1185.0 127.9 %all-reduce.19.cloned.1.call-done = f32[12,256,256]{2,1,0:T(8,128)} async-done(((f32[12,256,256]{2,1,0:T(8,128)}), f32[12,256,256]{2,1,0:T(8,128)}) %all-reduce.19.cloned.1.call-update) | async-done | bytes 3145744 | tf_op jit(solution)/shard_map/psum | solution.py:11
  1319.2 5.4 select_dynamic-update-slice_fusion.4
  1324.6 33.0 %all-reduce.21.cloned.1.call-done = f32[6,256,256]{2,1,0:T(8,128)} async-done(((f32[6,256,256]{2,1,0:T(8,128)}), f32[6,256,256]{2,1,0:T(8,128)}) %all-reduce.21.cloned.1.call-update) | async-done | bytes 1572880 | tf_op jit(solution)/shard_map/psum | solution.py:11
  1357.6 18.9 convolution_subtract_fusion.3
  1376.6 6.8 copy-done.2
  1388.8 27.5 %all-reduce.23.cloned.1.call-done = f32[256,256]{0,1:T(8,128)} async-done(((f32[256,256]{0,1:T(8,128)}), f32[256,256]{0,1:T(8,128)}) %all-reduce.23.cloned.1.call-update) | async-done | bytes 262160 | tf_op jit(solution)/shard_map/psum | solution.py:11
  1418.9 11.7 cholesky.290
  1430.7 9.8 custom-call.21
  1442.6 11.7 cholesky.307
  1458.5 3.9 while.16
  1463.1 20.6 custom-call.22
  1496.1 128.9 %all-reduce.25.cloned.1.call-done = f32[12,256,256]{2,1,0:T(8,128)} async-done(((f32[12,256,256]{2,1,0:T(8,128)}), f32[12,256,256]{2,1,0:T(8,128)}) %all-reduce.25.cloned.1.call-update) | async-done | bytes 3145744 | tf_op jit(solution)/shard_map/psum | solution.py:11
  1631.4 5.4 select_dynamic-update-slice_fusion.3
  1636.8 33.0 %all-reduce.27.cloned.1.call-done = f32[6,256,256]{2,1,0:T(8,128)} async-done(((f32[6,256,256]{2,1,0:T(8,128)}), f32[6,256,256]{2,1,0:T(8,128)}) %all-reduce.27.cloned.1.call-update) | async-done | bytes 1572880 | tf_op jit(solution)/shard_map/psum | solution.py:11
  1669.8 18.9 convolution_subtract_fusion.2
  1688.7 6.8 copy-done.1
  1701.0 27.5 %all-reduce.29.cloned.1.call-done = f32[256,256]{0,1:T(8,128)} async-done(((f32[256,256]{0,1:T(8,128)}), f32[256,256]{0,1:T(8,128)}) %all-reduce.29.cloned.1.call-update) | async-done | bytes 262160 | tf_op jit(solution)/shard_map/psum | solution.py:11
  1731.1 11.7 cholesky.324
  1742.8 9.8 custom-call.23
  1754.8 11.7 cholesky.341
  1775.3 20.6 custom-call.24
  1808.3 128.9 %all-reduce.31.cloned.1.call-done = f32[12,256,256]{2,1,0:T(8,128)} async-done(((f32[12,256,256]{2,1,0:T(8,128)}), f32[12,256,256]{2,1,0:T(8,128)}) %all-reduce.31.cloned.1.call-update) | async-done | bytes 3145744 | tf_op jit(solution)/shard_map/psum | solution.py:11
  1943.6 5.4 select_dynamic-update-slice_fusion.2
  1949.0 33.0 %all-reduce.33.cloned.1.call-done = f32[6,256,256]{2,1,0:T(8,128)} async-done(((f32[6,256,256]{2,1,0:T(8,128)}), f32[6,256,256]{2,1,0:T(8,128)}) %all-reduce.33.cloned.1.call-update) | async-done | bytes 1572880 | tf_op jit(solution)/shard_map/psum | solution.py:11
  1982.0 18.9 convolution_subtract_fusion.1
  2000.9 6.8 copy-done.3
  2013.2 27.5 %all-reduce.35.cloned.1.call-done = f32[256,256]{0,1:T(8,128)} async-done(((f32[256,256]{0,1:T(8,128)}), f32[256,256]{0,1:T(8,128)}) %all-reduce.35.cloned.1.call-update) | async-done | bytes 262160 | tf_op jit(solution)/shard_map/psum | solution.py:11
  2043.3 11.7 cholesky.358
  2055.0 9.8 custom-call.25
  2067.0 11.7 cholesky.375
  2087.5 20.6 custom-call.26
  2120.5 128.9 %all-reduce.37.cloned.1.call-done = f32[12,256,256]{2,1,0:T(8,128)} async-done(((f32[12,256,256]{2,1,0:T(8,128)}), f32[12,256,256]{2,1,0:T(8,128)}) %all-reduce.37.cloned.1.call-update) | async-done | bytes 3145744 | tf_op jit(solution)/shard_map/psum | solution.py:11
  2255.8 5.4 select_dynamic-update-slice_fusion.1
  2261.2 33.0 %all-reduce.39.cloned.1.call-done = f32[6,256,256]{2,1,0:T(8,128)} async-done(((f32[6,256,256]{2,1,0:T(8,128)}), f32[6,256,256]{2,1,0:T(8,128)}) %all-reduce.39.cloned.1.call-update) | async-done | bytes 1572880 | tf_op jit(solution)/shard_map/psum | solution.py:11
  2294.2 18.9 convolution_subtract_fusion
  2313.1 6.8 copy-done
  2325.2 27.7 %all-reduce.41.cloned.1.call-done = f32[256,256]{0,1:T(8,128)} async-done(((f32[256,256]{0,1:T(8,128)}), f32[256,256]{0,1:T(8,128)}) %all-reduce.41.cloned.1.call-update) | async-done | bytes 262160 | tf_op jit(solution)/shard_map/psum | solution.py:11
  2355.5 11.7 cholesky.392
  2367.2 9.8 custom-call.27
  2379.2 11.7 cholesky.409
  2399.6 20.9 custom-call.28
  2432.9 128.9 %all-reduce.43.cloned.1.call-done = f32[12,256,256]{2,1,0:T(8,128)} async-done(((f32[12,256,256]{2,1,0:T(8,128)}), f32[12,256,256]{2,1,0:T(8,128)}) %all-reduce.43.cloned.1.call-update) | async-done | bytes 3145744 | tf_op jit(solution)/shard_map/psum | solution.py:11
  2568.3 5.3 select_dynamic-update-slice_fusion
  2573.6 32.9 %all-reduce.45.cloned.1.call-done = f32[6,256,256]{2,1,0:T(8,128)} async-done(((f32[6,256,256]{2,1,0:T(8,128)}), f32[6,256,256]{2,1,0:T(8,128)}) %all-reduce.45.cloned.1.call-update) | async-done | bytes 1572880 | tf_op jit(solution)/shard_map/psum | solution.py:11
  2606.5 21.8 select_bitcast_fusion
  2628.3 44.5 %copy.167 = f32[12,1,256,6,1,256]{5,4,3,2,1,0:T(1,128)} copy(f32[12,1,256,6,1,256]{2,5,3,0,4,1:T(8,128)} %select_bitcast_fusion) | data formatting | bytes 37748736 | tf_op jit(solution)/shard_map/reshape | solution.py:100
  (280 shorter events, 196.3 us)
Async XLA Ops:
  6.5 645.3 %all-gather.2.cloned.1.call-start = ((), (), s32[]{:S(2)}) async-start(), calls=%async_computation.2 | async-start | bytes 37748736 | tf_op jit(solution)/shard_map/all_gather | solution.py:32
  11.2 0.7 copy-start.30
  13.0 709.6 %all-to-all-start = ((s32[4,1,4]{2,1,0:T(1,128)}), s32[4,1,4]{2,1,0:T(1,128)S(1)}, u32[]{:S(2)}, u32[]{:S(2)}) async-start(s32[4,1,4]{2,1,0:T(1,128)} %bitcast.3), calls=%async_computation | async-start | bytes 4096 | tf_op jit(solution)/shard_map/all_to_all | solution.py:68
  722.6 281.4 %all-to-all-start.1 = ((f32[4,4,256,6,256]{4,1,3,2,0:T(4,128)}), f32[4,4,256,6,256]{4,1,3,2,0:T(4,128)}, u32[]{:S(2)}, u32[]{:S(2)}) async-start(f32[4,4,256,6,256]{4,1,3,2,0:T(4,128)} %fusion.3), calls=%async_computation.1 | async-start | bytes 50331648 | tf_op jit(solution)/shard_map/all_to_all | solution.py:61
  731.0 373.0 %all-reduce.17.cloned.1.call-start = ((), (), s32[]{:S(2)}) async-start(), calls=%async_computation.3 | async-start | bytes 524288 | tf_op jit(solution)/shard_map/psum | solution.py:11
  1065.3 6.9 copy-start.4
  1072.9 240.0 %all-reduce.19.cloned.1.call-start = ((), (), s32[]{:S(2)}) async-start(), calls=%async_computation.4 | async-start | bytes 6291456 | tf_op jit(solution)/shard_map/psum | solution.py:11
  1073.0 1.9 slice-start.4
  1077.7 94.9 %copy-start.11 = (f32[12,256,1,256]{3,1,0,2:T(8,128)S(1)}, f32[12,256,1,256]{3,1,0,2:T(8,128)}, u32[]{:S(2)}) copy-start(f32[12,256,1,256]{3,1,0,2:T(8,128)} %copy.129) | copy-start | bytes 9437188
  1106.9 0.7 copy-start.20
  1143.1 2.4 copy-start.15
  1151.3 0.7 copy-start.26
  1184.9 172.8 %all-reduce.21.cloned.1.call-start = ((), (), s32[]{:S(2)}) async-start(), calls=%async_computation.5 | async-start | bytes 3145728 | tf_op jit(solution)/shard_map/psum | solution.py:11
  1315.7 100.7 %all-reduce.23.cloned.1.call-start = ((), (), s32[]{:S(2)}) async-start(), calls=%async_computation.6 | async-start | bytes 524288 | tf_op jit(solution)/shard_map/psum | solution.py:11
  1319.2 38.4 %copy-start.5 = (f32[12,256,256]{2,1,0:T(8,128)S(1)}, f32[12,256,256]{2,1,0:T(8,128)}, u32[]{:S(2)}) copy-start(f32[12,256,256]{2,1,0:T(8,128)} %all-reduce.19.cloned.1.call-done) | copy-start | bytes 9437188
  1376.5 6.9 copy-start.2
  1384.1 240.9 %all-reduce.25.cloned.1.call-start = ((), (), s32[]{:S(2)}) async-start(), calls=%async_computation.7 | async-start | bytes 6291456 | tf_op jit(solution)/shard_map/psum | solution.py:11
  1384.2 1.9 slice-start.2
  1388.8 94.9 %copy-start.12 = (f32[12,256,1,256]{3,1,0,2:T(8,128)S(1)}, f32[12,256,1,256]{3,1,0,2:T(8,128)}, u32[]{:S(2)}) copy-start(f32[12,256,1,256]{3,1,0,2:T(8,128)} %copy.137) | copy-start | bytes 9437188
  1418.2 0.7 copy-start.21
  1454.4 2.4 copy-start.16
  1462.4 0.7 copy-start.27
  1496.1 173.8 %all-reduce.27.cloned.1.call-start = ((), (), s32[]{:S(2)}) async-start(), calls=%async_computation.8 | async-start | bytes 3145728 | tf_op jit(solution)/shard_map/psum | solution.py:11
  1627.9 100.7 %all-reduce.29.cloned.1.call-start = ((), (), s32[]{:S(2)}) async-start(), calls=%async_computation.9 | async-start | bytes 524288 | tf_op jit(solution)/shard_map/psum | solution.py:11
  1631.4 38.4 %copy-start.6 = (f32[12,256,256]{2,1,0:T(8,128)S(1)}, f32[12,256,256]{2,1,0:T(8,128)}, u32[]{:S(2)}) copy-start(f32[12,256,256]{2,1,0:T(8,128)} %all-reduce.25.cloned.1.call-done) | copy-start | bytes 9437188
  1688.7 6.9 copy-start.1
  1696.3 240.9 %all-reduce.31.cloned.1.call-start = ((), (), s32[]{:S(2)}) async-start(), calls=%async_computation.10 | async-start | bytes 6291456 | tf_op jit(solution)/shard_map/psum | solution.py:11
  1696.4 1.9 slice-start.1
  1701.0 94.9 %copy-start.13 = (f32[12,256,1,256]{3,1,0,2:T(8,128)S(1)}, f32[12,256,1,256]{3,1,0,2:T(8,128)}, u32[]{:S(2)}) copy-start(f32[12,256,1,256]{3,1,0,2:T(8,128)} %copy.145) | copy-start | bytes 9437188
  1730.4 0.7 copy-start.22
  1766.6 2.4 copy-start.17
  1774.6 0.7 copy-start.28
  1808.2 173.8 %all-reduce.33.cloned.1.call-start = ((), (), s32[]{:S(2)}) async-start(), calls=%async_computation.11 | async-start | bytes 3145728 | tf_op jit(solution)/shard_map/psum | solution.py:11
  1940.1 100.7 %all-reduce.35.cloned.1.call-start = ((), (), s32[]{:S(2)}) async-start(), calls=%async_computation.12 | async-start | bytes 524288 | tf_op jit(solution)/shard_map/psum | solution.py:11
  1943.6 38.4 %copy-start.7 = (f32[12,256,256]{2,1,0:T(8,128)S(1)}, f32[12,256,256]{2,1,0:T(8,128)}, u32[]{:S(2)}) copy-start(f32[12,256,256]{2,1,0:T(8,128)} %all-reduce.31.cloned.1.call-done) | copy-start | bytes 9437188
  2000.9 6.9 copy-start.3
  2008.5 240.9 %all-reduce.37.cloned.1.call-start = ((), (), s32[]{:S(2)}) async-start(), calls=%async_computation.13 | async-start | bytes 6291456 | tf_op jit(solution)/shard_map/psum | solution.py:11
  2008.6 1.9 slice-start.3
  2013.2 94.9 %copy-start.14 = (f32[12,256,1,256]{3,1,0,2:T(8,128)S(1)}, f32[12,256,1,256]{3,1,0,2:T(8,128)}, u32[]{:S(2)}) copy-start(f32[12,256,1,256]{3,1,0,2:T(8,128)} %copy.153) | copy-start | bytes 9437188
  2042.6 0.7 copy-start.23
  2078.8 2.4 copy-start.18
  2086.8 0.7 copy-start.29
  2120.4 173.8 %all-reduce.39.cloned.1.call-start = ((), (), s32[]{:S(2)}) async-start(), calls=%async_computation.14 | async-start | bytes 3145728 | tf_op jit(solution)/shard_map/psum | solution.py:11
  2252.3 100.6 %all-reduce.41.cloned.1.call-start = ((), (), s32[]{:S(2)}) async-start(), calls=%async_computation.15 | async-start | bytes 524288 | tf_op jit(solution)/shard_map/psum | solution.py:11
  2255.8 38.4 %copy-start.8 = (f32[12,256,256]{2,1,0:T(8,128)S(1)}, f32[12,256,256]{2,1,0:T(8,128)}, u32[]{:S(2)}) copy-start(f32[12,256,256]{2,1,0:T(8,128)} %all-reduce.37.cloned.1.call-done) | copy-start | bytes 9437188
  2313.1 6.9 copy-start
  2320.7 241.1 %all-reduce.43.cloned.1.call-start = ((), (), s32[]{:S(2)}) async-start(), calls=%async_computation.16 | async-start | bytes 6291456 | tf_op jit(solution)/shard_map/psum | solution.py:11
  2320.8 1.9 slice-start
  2325.2 95.3 %copy-start.10 = (f32[12,256,1,256]{3,1,0,2:T(8,128)S(1)}, f32[12,256,1,256]{3,1,0,2:T(8,128)}, u32[]{:S(2)}) copy-start(f32[12,256,1,256]{3,1,0,2:T(8,128)} %copy.161) | copy-start | bytes 9437188
  2354.8 0.7 copy-start.24
  2391.0 2.4 copy-start.19
  2399.0 0.7 copy-start.25
  2432.8 173.7 %all-reduce.45.cloned.1.call-start = ((), (), s32[]{:S(2)}) async-start(), calls=%async_computation.17 | async-start | bytes 3145728 | tf_op jit(solution)/shard_map/psum | solution.py:11
  2568.3 38.3 %copy-start.9 = (f32[12,256,256]{2,1,0:T(8,128)S(1)}, f32[12,256,256]{2,1,0:T(8,128)}, u32[]{:S(2)}) copy-start(f32[12,256,256]{2,1,0:T(8,128)} %all-reduce.43.cloned.1.call-done) | copy-start | bytes 9437188
Sparse Core Ops, SparseCore 0:
  11.4 640.4 all-gather.1
  1073.0 31.0 all-reduce.16
  1185.0 127.7 all-reduce.18
  1315.8 41.7 all-reduce.20
  1384.3 32.0 all-reduce.22
  1496.2 128.7 all-reduce.24
  1628.0 41.7 all-reduce.26
  1696.4 32.0 all-reduce.28
  1808.4 128.8 all-reduce.30
  1940.2 41.7 all-reduce.32
  2008.6 32.0 all-reduce.34
  2120.6 128.8 all-reduce.36
  2252.4 41.7 all-reduce.38
  2320.8 32.0 all-reduce.40
  2433.0 128.8 all-reduce.42
  2564.7 41.7 all-reduce.44
where the time goes:
time: 2690 us; the launch traced here: 2680 us
  waiting for transfers between devices  1810 us (67%)
  other arithmetic  370 us (14%)
  local copies, waits for them, and re-layouts  235 us (9%)
  matrix products  233 us (9%)
    psum x15, waiting for transfers between devices, broadcast(): return lax.psum(jnp.where(mine, array, jnp.zeros_like(array)), axis)  945 us
    all_gather x1, waiting for transfers between devices, per_device(): shard_piece = lax.all_gather(children, 'pcol', axis=4, tiled=True)  634 us
    all_to_all x1, waiting for transfers between devices, per_device(): lax.all_to_all(jnp.einsum('dsr,ralb->dsalb', placement, sectioning, preci...  228 us
    another operation x35, other arithmetic, per_device(): factor = jnp.tril(jnp.linalg.cholesky(diagonal))  173 us
    another operation x16, other arithmetic, per_device(): lax.linalg.triangular_solve(factor, column, left_side=False, lower=True,...  122 us
    dot_general x5, matrix products, per_device(): jnp.einsum('rab,ceb->race', panel_left, panel_right, precision=highest)  97.4 us
    unnamed x64, local copies, waits for them, and re-layouts  91 us
  transfers between devices with their start and end apart: 18, of which 17 were waited for; matrix products, arithmetic and copies ran while one was open for 7% of the time, Pallas kernels for 0%

commit v1 on v0

v1 whole, which is shorter than its diff:
```python
import functools
import jax
import jax.numpy as jnp

from jax import lax
from jax.sharding import PartitionSpec as P
from jax.experimental import pallas as pl
from jax.experimental.pallas import tpu as pltpu

KB = 5
SUB = 64


def mm(a, b):
    return lax.dot_general(a, b, (((1,), (0,)), ((), ())),
        precision=lax.Precision.HIGHEST, preferred_element_type=jnp.float32)


def mm_t(a, b):
    return lax.dot_general(a, b, (((1,), (1,)), ((), ())),
        precision=lax.Precision.HIGHEST, preferred_element_type=jnp.float32)


def small_factor(block):
    n = block.shape[0]
    rows = lax.broadcasted_iota(jnp.int32, (n, 1), 0)
    lanes = lax.broadcasted_iota(jnp.int32, (n, 2 * n), 1)
    rows2 = lax.broadcasted_iota(jnp.int32, (n, 2 * n), 0)
    eye = jnp.where(lanes - n == rows2, 1.0, 0.0).astype(jnp.float32)
    aug = jnp.concatenate([block, jnp.zeros_like(block)], axis=1) + eye
    for j in range(n):
        row = aug[j : j + 1, :]
        col = aug[:, j : j + 1]
        scaled = row * (1.0 / row[:, j : j + 1])
        aug = aug - jnp.where(rows > j, col, 0.0) * scaled
    square = jnp.where(lanes == rows2, aug, 0.0)
    pivot = jnp.sum(square, axis=1, keepdims=True)
    aug = aug * (1.0 / jnp.sqrt(pivot))
    upper = jnp.where(lanes[:, :n] >= rows2[:, :n], aug[:, :n], 0.0)
    return upper.T, aug[:, n:]


def factor_kernel(a_ref, l_ref, w_ref, d_ref):
    count, size = a_ref.shape[0], a_ref.shape[2]
    parts = size // SUB
    l_ref[...] = a_ref[...]

    @pl.loop(0, count)
    def _(k):
        d_ref[...] = l_ref[k, k]
        w_ref[k] = jnp.zeros((size, size), jnp.float32)
        for t in range(parts):
            lo, hi = t * SUB, (t + 1) * SUB
            low, inv = small_factor(d_ref[lo:hi, lo:hi])
            d_ref[lo:hi, lo:hi] = low
            if t + 1 < parts:
                d_ref[lo:hi, hi:size] = jnp.zeros((SUB, size - hi), jnp.float32)
                below = mm_t(d_ref[hi:size, lo:hi], inv)
                d_ref[hi:size, lo:hi] = below
                d_ref[hi:size, hi:size] = d_ref[hi:size, hi:size] - mm_t(below, below)
            w_ref[k, lo:hi, lo:hi] = inv
            if t:
                w_ref[k, lo:hi, 0:lo] = -mm(inv, mm(d_ref[lo:hi, 0:lo], w_ref[k, 0:lo, 0:lo]))
        l_ref[k, k] = d_ref[...]

        @pl.loop(k + 1, count)
        def _(i):
            l_ref[i, k] = mm_t(l_ref[i, k], w_ref[k])

        @pl.loop(k + 1, count)
        def _(i):
            @pl.loop(k + 1, i + 1)
            def _(j):
                l_ref[i, j] = l_ref[i, j] - mm_t(l_ref[i, k], l_ref[j, k])


def factor(a):
    count, size = a.shape[0], a.shape[2]
    return pl.pallas_call(
        factor_kernel,
        out_shape=(jax.ShapeDtypeStruct(a.shape, jnp.float32),
                   jax.ShapeDtypeStruct((count, size, size), jnp.float32)),
        in_specs=[pl.BlockSpec(memory_space=pltpu.VMEM)],
        out_specs=(pl.BlockSpec(memory_space=pltpu.VMEM),) * 2,
        scratch_shapes=[pltpu.VMEM((size, size), jnp.float32)],
        compiler_params=pltpu.CompilerParams(vmem_limit_bytes=40 << 20),
    )(a)


def place_kernel(row_ref, hit_ref, sec_ref, slot_ref, front_ref, first_ref, second_ref, out_ref):
    r, c = pl.program_id(0), pl.program_id(1)
    cols = pl.num_programs(1)
    total = front_ref[0]
    zero = jnp.zeros_like(total)
    total = total + jnp.where(hit_ref[0, r * cols + c] > 0, first_ref[0, 0], zero)
    total = total + jnp.where(hit_ref[1, r * cols + c] > 0, second_ref[0, 0], zero)
    out_ref[0] = total


def place(front, received, source, hit, section, slot):
    rows, size, width = front.shape
    cols = width // size

    def child_map(k):
        return lambda r, c, s, h, x, y: (s[k, r * cols + c], x[k, r * cols + c], 0, y[k, r * cols + c])

    return pl.pallas_call(
        place_kernel,
        grid_spec=pltpu.PrefetchScalarGridSpec(
            num_scalar_prefetch=4,
            grid=(rows, cols),
            in_specs=[
                pl.BlockSpec((1, size, size), lambda r, c, s, h, x, y: (r, 0, c)),
                pl.BlockSpec((1, 1, size, size), child_map(0)),
                pl.BlockSpec((1, 1, size, size), child_map(1)),
            ],
            out_specs=pl.BlockSpec((1, size, size), lambda r, c, s, h, x, y: (r, 0, c)),
        ),
        out_shape=jax.ShapeDtypeStruct(front.shape, front.dtype),
    )(source, hit, section, slot, front, received, received)


def per_device(parent, children, index_maps):
    prow_count = lax.axis_size("prow")
    pcol_count = lax.axis_size("pcol")
    prow_id = lax.axis_index("prow")
    pcol_id = lax.axis_index("pcol")
    half = prow_count // 2
    size = parent.shape[2]
    rows, cols = parent.shape[0], parent.shape[3]
    child_rows, child_cols = children.shape[0], children.shape[3]
    child_blocks = index_maps.shape[1]
    high = lax.Precision.HIGH
    front = parent.reshape(rows, size, cols * size)
    child = children.reshape(child_rows, size, child_cols * size)

    blocks = jnp.arange(child_blocks)
    dest = index_maps % prow_count
    earlier = (blocks[:, None] > blocks[None, :]) & (blocks[:, None] % half == blocks[None, :] % half)
    position = jnp.sum(earlier[None] & (dest[:, :, None] == dest[:, None, :]), axis=2)
    most = (child_rows // 2 + 2) // 3 * (2 - min(1, half // 3))

    sections = [
        lax.ppermute(child, "pcol", [(q, (3 * q + d) % pcol_count) for q in range(pcol_count)])
        for d in range(3)
    ]
    mine = (blocks // half)[None, :] * 0 + blocks[None, :] % half
    here = (jnp.arange(2)[:, None] == prow_id // half) & (mine == prow_id % half)
    wanted = (
        here[None, None]
        & (dest[None, None] == jnp.arange(prow_count)[:, None, None, None])
        & (position[None, None] == jnp.arange(most)[None, :, None, None])
    )
    index = jnp.sum(jnp.where(wanted, (blocks // half)[None, None, None, :], 0), axis=(2, 3))
    index = index.reshape(-1)
    received = []
    for section in sections:
        packed = jnp.take(section, index, axis=0).reshape(prow_count, most, size, child_cols * size)
        got = lax.all_to_all(packed, "prow", split_axis=0, concat_axis=0, tiled=True)
        received.append(got.reshape(prow_count * most, size, child_cols * size))
    received = jnp.stack(received, axis=1)

    row_ids = jnp.arange(rows) * prow_count + prow_id
    col_ids = jnp.arange(cols) * pcol_count + pcol_id

    def lookup(table, at):
        return jnp.sum(jnp.where(at[None, :, None] == blocks[None, None, :], table[:, None, :], 0), axis=2)

    u, v = row_ids // 3, col_ids // 3
    hit = (lookup(index_maps, u) == row_ids[None])[:, :, None] & (lookup(index_maps, v) == col_ids[None])[:, None, :]
    holder = jnp.arange(2)[:, None] * half + (u % half)[None, :]
    source = (holder * most + lookup(position, u))[:, :, None]
    shape = (2, rows, cols)
    source = jnp.where(hit, source, 0)
    section_id = jnp.where(hit, (col_ids % 3)[None, None, :], 0)
    slot = jnp.where(hit, (v // pcol_count)[None, None, :], 0)
    flat = lambda x: jnp.broadcast_to(x, shape).reshape(2, rows * cols).astype(jnp.int32)
    front = place(front, received, flat(source), flat(hit), flat(section_id), flat(slot))

    lead = -(-KB // prow_count)
    tops = lax.all_gather(front[:lead], "prow", axis=1, tiled=False)
    tops = tops.reshape(lead * prow_count, size, cols * size)[:KB]
    lefts = lax.all_gather(front[:, :, :size], "pcol", axis=0, tiled=False)[:KB]
    corner = lax.all_gather(tops[:, :, :size], "pcol", axis=1, tiled=False)[:, :KB]
    lower, inverse = factor(corner)

    left_x, top_x = [], []
    for k in range(KB):
        left, top = lefts[k].reshape(rows * size, size), tops[k]
        for m in range(k):
            left = left - lax.dot_general(left_x[m], lower[k, m], (((1,), (1,)), ((), ())), precision=high)
            top = top - jnp.dot(lower[k, m], top_x[m], precision=high)
        left_x.append(lax.dot_general(left, inverse[k], (((1,), (1,)), ((), ())), precision=high))
        top_x.append(jnp.dot(inverse[k], top, precision=high))
    left_all = jnp.concatenate(left_x, axis=1)
    top_all = jnp.concatenate(top_x, axis=0)
    front = front - jnp.dot(left_all, top_all, precision=high).reshape(rows, size, cols * size)

    column = jnp.zeros((rows, size, size), jnp.float32)
    for k in range(KB):
        column = jnp.where(pcol_id == k, left_x[k].reshape(rows, size, size), column)
        for m in range(k, KB):
            at = (row_ids == m) & (pcol_id == k)
            column = jnp.where(at[:, None, None], lower[m, k][None], column)
        above = (row_ids < k) & (pcol_id == k)
        column = jnp.where(above[:, None, None], 0.0, column)
    front = jnp.where((row_ids < KB)[:, None, None], 0.0, front)
    first = jnp.where(pcol_id < KB, column, front[:, :, :size])
    front = jnp.concatenate([first, front[:, :, size:]], axis=2)
    return front.reshape(rows, 1, size, cols, 1, size)


def solution(mesh):
    spec = P(None, "prow", None, None, "pcol", None)
    return jax.shard_map(
        per_device, mesh=mesh, in_specs=(spec, spec, P()), out_specs=spec, check_vma=False
    )
```

time: 2690 us -> 1700 us (0.63)
  waiting for transfers between devices: 1810 us -> 780 us
  blocking collectives: 0 us -> 198 us
  Pallas kernels: 0 us -> 181 us
  other arithmetic: 370 us -> 205 us
  matrix products: 233 us -> 110 us
  local copies, waits for them, and re-layouts: 235 us -> 159 us
  starting transfers between devices: 13.3 us -> 41.4 us
    psum x15 -> x0, waiting for transfers between devices: 945 us -> none  [broadcast(): return lax.psum(jnp.where(mine, array, jnp.zeros_like(array)), axis)]
    another operation x51 -> x1, other arithmetic: 294 us -> 18 us  [per_device(): received = jnp.stack(received, axis=1)]
    all_to_all x2 -> x1, waiting for transfers between devices: 228 us -> 0.01 us  [per_device(): lax.all_to_all(packed, 'prow', split_axis=0, concat_axis=0, tiled=True)]
    all_to_all x0 -> x2, blocking collectives: none -> 198 us  [per_device(): lax.all_to_all(packed, 'prow', split_axis=0, concat_axis=0, tiled=True)]
    pallas_call x0 -> x2, Pallas kernels: none -> 181 us  [the longest x1 136 us: factor(): pl.pallas_call(factor_kernel, out_shape=(jax.ShapeDtypeStruct(a.shape, jn...]
    unnamed x0 -> x4, other arithmetic: none -> 124 us
    ppermute x0 -> x3, waiting for transfers between devices: none -> 86.3 us  [per_device(): lax.ppermute(child, 'pcol', [(q, (3 * q + d) % pcol_count) for q in range...]
    unnamed x64 -> x36, local copies, waits for them, and re-layouts: 91 us -> 5.5 us
  transfers between devices with their start and end apart: 18 -> 7, of which waited for: 17 -> 4; matrix products, arithmetic and copies ran while one was open for 7% -> 11% of each run, Pallas kernels for 0% -> 8%
where the time goes in v1:
time: 1700 us; the launch traced here: 1690 us
  waiting for transfers between devices  780 us (46%)
  other arithmetic  205 us (12%)
  blocking collectives  198 us (12%)
  Pallas kernels  181 us (11%)
  local copies, waits for them, and re-layouts  159 us (9%)
  matrix products  110 us (6%)
  starting transfers between devices  41.4 us (2%)
    all_gather x1, waiting for transfers between devices, per_device(): lefts = lax.all_gather(front[:, :, :size], 'pcol', axis=0, tiled=False)[:KB]  312 us
    all_gather x1, waiting for transfers between devices, per_device(): tops = lax.all_gather(front[:lead], 'prow', axis=1, tiled=False)  235 us
    all_to_all x2, blocking collectives, per_device(): lax.all_to_all(packed, 'prow', split_axis=0, concat_axis=0, tiled=True)  198 us
    all_gather x1, waiting for transfers between devices, per_device(): lax.all_gather(tops[:, :, :size], 'pcol', axis=1, tiled=False)[:, :KB]  147 us
    pallas_call x1, Pallas kernels, factor(): pl.pallas_call(factor_kernel, out_shape=(jax.ShapeDtypeStruct(a.shape, jn...  136 us
    unnamed x4, other arithmetic  124 us
    ppermute x3, waiting for transfers between devices, per_device(): lax.ppermute(child, 'pcol', [(q, (3 * q + d) % pcol_count) for q in range...  86.3 us
    pallas_call x1, Pallas kernels, place(): pl.pallas_call(place_kernel, grid_spec=pltpu.PrefetchScalarGridSpec(num_s...  45.3 us
  transfers between devices with their start and end apart: 7, of which 4 were waited for; matrix products, arithmetic and copies ran while one was open for 11% of the time, Pallas kernels for 8%

profile of v1, /device:TPU:0, one launch (start us, length us, event | category | flops | bytes accessed | tf_op | source)
XLA Modules:
  0.0 1689.1 jit_solution(689977031564360352)
XLA Ops:
  6.5 15.9 reduce.1
  22.4 6.4 reshape.500
  28.9 33.1 %collective-permute-start = (f32[8,256,512]{2,1,0:T(8,128)}, f32[8,256,512]{2,1,0:T(8,128)}, u32[]{:S(2)}, u32[]{:S(2)}) collective-permute-start(f32[8,256,512]{2,1,0:T(8,128)} %reshape.500), channel_id=1, source_target_pairs={{0,0},{1,3},{2,6},{3,1},{4,4},{5,7},{6,2},{7,5},{8,8},{9,11},{10,1... | collective-permute-start | bytes 12582920 | tf_op jit(solution)/shard_map/ppermute | solution.py:144
  62.0 1.9 collective-permute-start.2
  64.6 6.7 gather_fusion
  71.3 86.3 %collective-permute-done.1 = f32[8,256,512]{2,1,0:T(8,128)} collective-permute-done((f32[8,256,512]{2,1,0:T(8,128)}, f32[8,256,512]{2,1,0:T(8,128)}, u32[]{:S(2)}, u32[]{:S(2)}) %collective-permute-start.1) | collective-permute-done | bytes 4194336 | tf_op jit(solution)/shard_map/ppermute | solution.py:144
  157.5 6.6 gather_fusion.1
  164.1 6.6 gather_fusion.2
  170.6 18.0 %broadcast_select_fusion.2 = (f32[16,256,512]{2,1,0:T(8,128)}, f32[16,256,512]{2,1,0:T(8,128)}, f32[16,256,512]{2,1,0:T(8,128)}) fusion(f32[16,256,512]{2,1,0:T(8,128)} %gather_fusion, pred[16]{0:T(512)(128)(4,1)S(1)} %compare_and_fusion.1, f32[16,256,512]{2,1,0:T(8,128)} %gather_fusion.1, f32[16,256,512]{2,1,0:T(8,128)} %gather_fusion.2), kind=kLoop, calls=%fused_computation.8 | loop fusion | flops 6291456 | bytes 50331664 | tf_op jit(solution)/shard_map/jit(_take)/select_n | solution.py:158
  188.6 101.2 %all_to_all.15 = f32[4,4,256,512]{3,2,1,0:T(8,128)} all-to-all(f32[4,4,256,512]{3,2,1,0:T(8,128)} %bitcast.174), channel_id=1, replica_groups=mesh['prow'=4,'pcol'=8] {'prow'}, dimensions={0} | all-to-all | bytes 16777216 | tf_op jit(solution)/shard_map/all_to_all | solution.py:159
  289.8 96.9 %all_to_all.16 = f32[4,4,256,512]{3,2,1,0:T(8,128)} all-to-all(f32[4,4,256,512]{3,2,1,0:T(8,128)S(1)} %bitcast.173), channel_id=1, replica_groups=mesh['prow'=4,'pcol'=8] {'prow'}, dimensions={0} | all-to-all | bytes 16777216 | tf_op jit(solution)/shard_map/all_to_all | solution.py:159
  386.7 5.6 all-to-all-start.2
  395.3 108.4 %reduce = f32[12,256,6,256]{3,2,1,0:T(8,128)} reduce(f32[12,1,256,6,1,256]{5,4,3,2,1,0:T(1,128)} %param.5, f32[]{:T(128)} %constant.146), dimensions={1,4}, to_apply=%param.5.reduce_sub_computation | reduce | bytes 37748740 | tf_op args[0]
  503.7 24.3 %reshape.499.front_ref = f32[12,256,1536]{2,1,0:T(8,128)} reshape(f32[12,256,6,256]{3,2,1,0:T(8,128)} %reduce) | data formatting | bytes 37748736 | tf_op jit(solution)/shard_map/reshape | solution.py:134
  528.6 18.0 %pad_maximum_fusion.first_ref.second_ref = f32[16,3,256,512]{3,2,1,0:T(8,128)} fusion(f32[16,1,256,512]{3,2,1,0:T(8,128)} %bitcast.5, f32[16,1,256,512]{3,2,1,0:T(8,128)} %bitcast.176, f32[16,1,256,512]{3,2,1,0:T(8,128)} %bitcast.175), kind=kLoop, calls=%fused_computation.3 | loop fusion | flops 12582912 | bytes 50331648 | tf_op jit(solution)/shard_map/stack | solution.py:161
  546.6 45.3 %shard_map.37 = f32[12,256,1536]{2,1,0:T(8,128)} custom-call(s32[2,72]{1,0:T(2,128)} %get-tuple-element.39.row_ref, s32[2,72]{1,0:T(2,128)} %convert_element_type.7.hit_ref, s32[2,72]{1,0:T(2,128)} %get-tuple-element.38.sec_ref, s32[2,72]{1,0:T(2,128)} %get-tuple-element.37.slot_ref, f32[12,256,1536]{2,1,0:T(8,128)} %reshape.499.front_ref, ...), custom_call_target="tpu_custom_call" | custom-call | tf_op jit(solution)/shard_map/pallas_call | solution.py:107
  591.9 3.8 slice.193
  595.7 235.0 %all-gather.7.cloned.1.call-done = f32[2,1024,1536]{2,1,0:T(8,128)} async-done(((f32[2,256,1536]{2,1,0:T(8,128)}), f32[2,1024,1536]{2,1,0:T(8,128)}) %all-gather.7.cloned.1.call-update) | async-done | bytes 12582928 | tf_op jit(solution)/shard_map/all_gather | solution.py:181
  830.7 2.5 slice.194
  833.4 3.8 slice.196
  837.4 146.8 %all-gather.9.cloned.1.call-done = f32[5,2048,256]{2,1,0:T(8,128)} async-done(((f32[5,256,256]{2,1,0:T(8,128)}), f32[5,2048,256]{2,1,0:T(8,128)}) %all-gather.9.cloned.1.call-update) | async-done | bytes 10485776 | tf_op jit(solution)/shard_map/all_gather | solution.py:184
  984.2 3.5 slice.195.a_ref
  987.7 135.7 %shard_map.38 = (f32[5,5,256,256]{3,2,1,0:T(8,128)S(1)}, f32[5,256,256]{2,1,0:T(8,128)S(1)}) custom-call(f32[5,5,256,256]{3,2,1,0:T(8,128)S(1)} %slice.195.a_ref), custom_call_target="tpu_custom_call" | custom-call | tf_op jit(solution)/shard_map/pallas_call | solution.py:79
  1123.4 4.6 constant_dynamic-update-slice_fusion.8
  1128.0 2.2 convolution_subtract_fusion.13
  1130.2 2.2 convolution_subtract_fusion.19
  1132.5 2.2 convolution_subtract_fusion.18
  1134.7 2.2 convolution_subtract_fusion.16
  1136.9 2.0 constant_dynamic-update-slice_fusion.7
  1139.0 0.8 convolution_subtract_fusion.12
  1139.8 0.8 convolution_subtract_fusion.17
  1140.6 0.8 convolution_subtract_fusion.15
  1141.5 2.0 constant_dynamic-update-slice_fusion.6
  1143.5 0.8 convolution_subtract_fusion.11
  1144.3 0.8 convolution_subtract_fusion.14
  1145.1 2.1 constant_dynamic-update-slice_fusion.5
  1147.2 0.8 convolution_subtract_fusion.10
  1148.0 2.4 convolution_dynamic-update-slice_fusion
  1150.5 1.9 slice_bitcast_fusion.20
  1152.4 312.1 %all-gather.11.cloned.1.call-done = f32[96,256,256]{2,1,0:T(8,128)} async-done(((f32[12,256,256]{2,1,0:T(8,128)}), f32[96,256,256]{2,1,0:T(8,128)}) %all-gather.11.cloned.1.call-update) | async-done | bytes 25165840 | tf_op jit(solution)/shard_map/all_gather | solution.py:183
  1464.5 11.2 fusion.32
  1475.7 5.1 broadcast_select_fusion.3
  1480.8 2.5 convolution_subtract_fusion.9
  1483.4 2.5 convolution_subtract_fusion.8
  1485.9 2.4 convolution_subtract_fusion.6
  1488.3 1.4 constant_dynamic-update-slice_fusion.3
  1489.8 2.6 convolution_subtract_fusion.7
  1492.4 2.7 convolution_subtract_fusion.5
  1495.1 2.4 convolution_subtract_fusion.3
  1497.5 2.4 convolution_subtract_fusion.2
  1499.9 1.4 constant_dynamic-update-slice_fusion.2
  1501.3 2.6 convolution_subtract_fusion.4
  1504.0 2.4 convolution_subtract_fusion.1
  1506.4 1.4 constant_dynamic-update-slice_fusion.1
  1507.8 5.4 copy-done.9
  1513.3 2.7 convolution_subtract_fusion
  1515.9 4.2 constant_dynamic-update-slice_fusion
  1520.2 44.5 %fusion.33 = f32[3072,1536]{1,0:T(8,128)} fusion(f32[3072,1280]{1,0:T(8,128)} %get-tuple-element.47, f32[1280,1536]{1,0:T(8,128)} %convolution_dynamic-update-slice_fusion), kind=kOutput, calls=%fused_computation.162 | convolution fusion | flops 36238786560 | bytes 42467328 | tf_op jit(solution)/shard_map/dot_general | solution.py:197
  1564.7 14.2 subtract_select_fusion
  1579.0 12.0 slice.208
  1591.0 15.3 slice_select_fusion
  1606.3 12.7 pad_maximum_fusion.1
  1619.0 18.6 %copy.17 = f32[12,256,1536]{1,2,0:T(8,128)} copy(f32[12,256,1536]{2,1,0:T(8,128)} %pad_maximum_fusion.1) | data formatting | bytes 37748736 | tf_op jit(solution)/shard_map/concatenate | solution.py:209
  1637.6 44.5 %copy.18 = f32[12,1,256,6,1,256]{5,4,3,2,1,0:T(1,128)} copy(f32[12,1,256,6,1,256]{2,5,3,0,4,1:T(8,128)} %bitcast.168) | data formatting | bytes 37748736 | tf_op jit(solution)/shard_map/reshape | solution.py:210
  (98 shorter events, 4.6 us)
Async XLA Ops:
  22.4 41.5 %copy-start.10 = (s32[2,16]{1,0:T(2,128)S(1)}, s32[2,16]{1,0:T(2,128)}, u32[]{:S(2)}) copy-start(s32[2,16]{1,0:T(2,128)} %param.7) | copy-start | bytes 388
  28.9 35.7 %collective-permute-start = (f32[8,256,512]{2,1,0:T(8,128)}, f32[8,256,512]{2,1,0:T(8,128)}, u32[]{:S(2)}, u32[]{:S(2)}) collective-permute-start(f32[8,256,512]{2,1,0:T(8,128)} %reshape.500), channel_id=1, source_target_pairs={{0,0},{1,3},{2,6},{3,1},{4,4},{5,7},{6,2},{7,5},{8,8},{9,11},{10,1... | collective-permute-start | bytes 12582920 | tf_op jit(solution)/shard_map/ppermute | solution.py:144
  61.9 95.6 %collective-permute-start.1 = (f32[8,256,512]{2,1,0:T(8,128)}, f32[8,256,512]{2,1,0:T(8,128)}, u32[]{:S(2)}, u32[]{:S(2)}) collective-permute-start(f32[8,256,512]{2,1,0:T(8,128)} %reshape.500), channel_id=1, source_target_pairs={{0,1},{1,4},{2,7},{3,2},{4,5},{5,0},{6,3},{7,6},{8,9},{9,12},{10,1... | collective-permute-start | bytes 12582920 | tf_op jit(solution)/shard_map/ppermute | solution.py:144
  62.0 102.1 %collective-permute-start.2 = (f32[8,256,512]{2,1,0:T(8,128)}, f32[8,256,512]{2,1,0:T(8,128)}, u32[]{:S(2)}, u32[]{:S(2)}) collective-permute-start(f32[8,256,512]{2,1,0:T(8,128)} %reshape.500), channel_id=1, source_target_pairs={{0,2},{1,5},{2,0},{3,3},{4,6},{5,1},{6,4},{7,7},{8,10},{9,13},{10,... | collective-permute-start | bytes 12582920 | tf_op jit(solution)/shard_map/ppermute | solution.py:144
  188.6 101.2 %slice-start.5 = ((s8[8388608]{0:T(1024)(128)(4,1)}), s8[4194304]{0:T(1024)(128)(4,1)S(1)}, s32[]{:S(2)}) async-start(s8[8388608]{0:T(1024)(128)(4,1)} %bitcast.171), calls=%async_computation.11 | async-start | bytes 8388608
  188.6 101.2 %slice-start.6 = ((s8[8388608]{0:T(1024)(128)(4,1)}), s8[4194304]{0:T(1024)(128)(4,1)S(1)}, s32[]{:S(2)}) async-start(s8[8388608]{0:T(1024)(128)(4,1)} %bitcast.171), calls=%async_computation.12 | async-start | bytes 8388608
  386.7 141.9 %all-to-all-start.2 = ((f32[4,4,256,512]{3,2,1,0:T(8,128)}), f32[4,4,256,512]{3,2,1,0:T(8,128)}, u32[]{:S(2)}, u32[]{:S(2)}) async-start(f32[4,4,256,512]{3,2,1,0:T(8,128)} %bitcast.170), calls=%async_computation.2 | async-start | bytes 16777216 | tf_op jit(solution)/shard_map/all_to_all | solution.py:159
  392.4 438.3 %all-gather.7.cloned.1.call-start = ((), (), s32[]{:S(2)}) async-start(), calls=%async_computation.3 | async-start | bytes 15728640 | tf_op jit(solution)/shard_map/all_gather | solution.py:181
  595.7 388.5 %all-gather.9.cloned.1.call-start = ((), (), s32[]{:S(2)}) async-start(), calls=%async_computation.4 | async-start | bytes 11796480 | tf_op jit(solution)/shard_map/all_gather | solution.py:184
  833.2 631.3 %all-gather.11.cloned.1.call-start = ((), (), s32[]{:S(2)}) async-start(), calls=%async_computation.5 | async-start | bytes 28311552 | tf_op jit(solution)/shard_map/all_gather | solution.py:183
  1123.4 27.0 %copy-start = (f32[5,5,256,256]{3,2,1,0:T(8,128)}, f32[5,5,256,256]{3,2,1,0:T(8,128)S(1)}, u32[]{:S(2)}) copy-start(f32[5,5,256,256]{3,2,1,0:T(8,128)S(1)} %get-tuple-element.8) | copy-start | bytes 19660804
  1475.7 5.1 copy-start.8
  1480.8 2.5 copy-start.7
  1483.3 2.6 copy-start.6
  1489.8 7.7 copy-start.1
  1492.4 2.7 copy-start.5
  1501.3 2.6 copy-start.3
  1507.8 5.4 copy-start.9
  1513.3 2.7 copy-start.4
  1515.9 48.7 %slice-start = ((s8[18874368]{0:T(1024)(128)(4,1)}), s8[4194304]{0:T(1024)(128)(4,1)S(1)}, s32[]{:S(2)}) async-start(s8[18874368]{0:T(1024)(128)(4,1)} %bitcast.165), calls=%async_computation.6 | async-start | bytes 8388608
  1520.2 44.5 %slice-start.1 = ((s8[18874368]{0:T(1024)(128)(4,1)}), s8[4194304]{0:T(1024)(128)(4,1)S(1)}, s32[]{:S(2)}) async-start(s8[18874368]{0:T(1024)(128)(4,1)} %bitcast.165), calls=%async_computation.7 | async-start | bytes 8388608
  1520.2 44.5 %slice-start.2 = ((s8[18874368]{0:T(1024)(128)(4,1)}), s8[4194304]{0:T(1024)(128)(4,1)S(1)}, s32[]{:S(2)}) async-start(s8[18874368]{0:T(1024)(128)(4,1)} %bitcast.165), calls=%async_computation.8 | async-start | bytes 8388608
  1520.2 44.5 %slice-start.3 = ((s8[18874368]{0:T(1024)(128)(4,1)}), s8[4194304]{0:T(1024)(128)(4,1)S(1)}, s32[]{:S(2)}) async-start(s8[18874368]{0:T(1024)(128)(4,1)} %bitcast.165), calls=%async_computation.9 | async-start | bytes 8388608
  1520.2 44.5 %slice-start.4 = ((s8[18874368]{0:T(1024)(128)(4,1)}), s8[2097152]{0:T(1024)(128)(4,1)S(1)}, s32[]{:S(2)}) async-start(s8[18874368]{0:T(1024)(128)(4,1)} %bitcast.165), calls=%async_computation.10 | async-start | bytes 4194304
  1578.9 12.1 copy-start.2
Sparse Core Ops, SparseCore 0:
  595.8 234.8 all-gather.6
  833.3 150.8 all-gather.8
  985.7 478.6 all-gather.10
